TPU v7x, 32 devices: a whole 2x2x4 slice. The times are simulated.
32 devices in a mesh: cfg: 2 (over y), tm: 4 (over z), space: 2 (over x), spin: 2 (over core).
Axes of the slice: x: 2, y: 2, z: 4, core: 2. Of those that a mesh axis runs over, the one named last changes fastest.
Arguments:
- eigenvectors: bfloat16 [16, 2048, 3, 128], P(('cfg', 'tm'), ('space', 'spin')), parts along dimension 0, may hold values from -1.25 to 1.25
- momenta: int32 [8, 3], replicated, may hold values from -2 to 2, as said below
- time_pairs: int32 [32, 2], P(('cfg', 'tm')), parts along dimension 0, may hold values from 0 to 7
- slot_map: int32 [8], replicated, may hold values from 0 to 7, each once
- perambulators: bfloat16 [32, 64, 2048], P(('cfg', 'tm')), parts along dimension 0, may hold values from -0.046875 to 0.046875
Outputs:
- meson_loops: bfloat16 [32, 8, 64, 16, 128], P(('cfg', 'tm'), None, ('space', 'spin')), parts along dimension 0
There are 2 independent parts, one for each index of `cfg`. A program takes and returns all parts, laid end to end along the dimension named above; an argument that names none is the same for every part. Nothing has to cross between parts.
Inputs may be any that keep to these rules, and one draw needn't show every extreme that they name: `momenta`: every momentum row has a component that is not zero. slot_map is a permutation of the 8 stored rows.
All inputs are finite; a program needn't handle non-finite values.
Results may differ from a plain program's by a relative error of at most 0.0074.
Values may be sent and summed in bfloat16 or wider, within the bound.
A program may use at most 64 MiB of HBM per device.

v0:
```python
import jax
import jax.numpy as jnp
from jax import lax
from jax.sharding import PartitionSpec as P

LAT = 32


TURN = 6.283185307179586


def elemental(time_slab, momenta, first_site):
    site_count = time_slab.shape[0]
    vectors = time_slab.shape[2] // 2
    site_ids = first_site + lax.iota(jnp.int32, site_count)
    coord_x = site_ids % LAT
    coord_y = site_ids // LAT % LAT
    coord_z = site_ids // (LAT * LAT)
    real_part = time_slab[:, :, :vectors].astype(jnp.float32)
    imag_part = time_slab[:, :, vectors:].astype(jnp.float32)
    conj_left = time_slab.reshape(site_count * 6, vectors)
    results = []
    for momentum_row in range(momenta.shape[0]):
        wavenum = jnp.mod(
            momenta[momentum_row, 0] * coord_x
            + momenta[momentum_row, 1] * coord_y
            + momenta[momentum_row, 2] * coord_z,
            LAT,
        )
        angles = wavenum.astype(jnp.float32) * (TURN / LAT)
        cosine = jnp.cos(angles)[:, None, None]
        sines = jnp.sin(angles)[:, None, None]
        turned_real = cosine * real_part - sines * imag_part
        turned_imag = sines * real_part + cosine * imag_part
        upper_rows = jnp.concatenate([turned_real, turned_imag], axis=-1)
        lower_rows = jnp.concatenate([turned_imag, -turned_real], axis=-1)
        phased = (
            jnp.stack([upper_rows, lower_rows], axis=2)
            .reshape(site_count * 6, 2 * vectors)
            .astype(jnp.bfloat16)
        )
        results.append(
            lax.dot_general(
                conj_left, phased, (((0,), (0,)), ((), ())), preferred_element_type=jnp.float32
            )
        )
    return jnp.stack(results)


def contract(sink_rows, source_full, perambulators):
    pair_count, moms, share_rows, width = sink_rows.shape
    vectors = width // 2
    parts = perambulators.reshape(pair_count, vectors, 16, 2, vectors)
    lower = jnp.stack([-parts[:, :, :, 1], parts[:, :, :, 0]], axis=3).reshape(
        pair_count, vectors, 32 * vectors
    )
    right_side = jnp.concatenate([perambulators, lower], axis=1)
    left_side = sink_rows.reshape(pair_count, moms * share_rows, width)
    halfway = jnp.einsum(
        "kmx,kxc->kmc", left_side, right_side, preferred_element_type=jnp.float32
    ).astype(jnp.bfloat16)
    halfway = halfway.reshape(pair_count, moms, share_rows * 16, width)
    source_parts = source_full.reshape(pair_count, moms, vectors, 2, vectors)
    swapped = jnp.stack([-source_parts[:, :, :, 1], source_parts[:, :, :, 0]], axis=3).reshape(
        pair_count, moms, vectors, width
    )
    conjugate = jnp.stack([source_full, swapped], axis=2).reshape(pair_count, moms, width, width)
    loops = jnp.einsum("kpmx,kpnx->kpmn", halfway, conjugate, preferred_element_type=jnp.float32)
    return loops.astype(jnp.bfloat16).reshape(pair_count, moms, share_rows, 16, width)


def picker(targets, offset, number):
    return (targets[:, None] == offset + lax.iota(jnp.int32, number)[None, :]).astype(jnp.bfloat16)


def per_device(eigenvectors, momenta, time_pairs, slot_map, perambulators):
    groups = lax.axis_size(("space", "spin"))
    position = lax.axis_index(("space", "spin"))
    site_count = eigenvectors.shape[1]
    vectors = perambulators.shape[1]
    share_rows = vectors // groups
    pair_count = time_pairs.shape[0]
    moms = momenta.shape[0]
    width = 2 * vectors
    partial_value = lax.map(
        lambda time_slab: elemental(time_slab, momenta, position * site_count), eigenvectors
    )
    sink_slot = slot_map[time_pairs[:, 0]]
    source_slot = slot_map[time_pairs[:, 1]]
    row_share = lax.psum_scatter(
        partial_value, ("space", "spin"), scatter_dimension=2, tiled=True
    ).astype(jnp.bfloat16)
    initial = (
        jnp.zeros((pair_count, moms * share_rows * width), jnp.float32),
        jnp.zeros((pair_count, moms * share_rows * width), jnp.float32),
    )
    arrived = jax.tree.map(lambda part: lax.all_gather(part, "tm", axis=0, tiled=True), row_share)
    anchor = jnp.int32(0)
    number = arrived.shape[0]
    flat = arrived.reshape(number, -1)
    sink_acc = initial[0] + jnp.dot(
        picker(sink_slot, anchor, number), flat, preferred_element_type=jnp.float32
    )
    source_acc = initial[1] + jnp.dot(
        picker(source_slot, anchor, number), flat, preferred_element_type=jnp.float32
    )
    sink_rows = sink_acc.astype(jnp.bfloat16).reshape(pair_count, moms, share_rows, width)
    source_share = source_acc.astype(jnp.bfloat16).reshape(pair_count, moms, share_rows, width)
    source_full = lax.all_gather(source_share, ("space", "spin"), axis=2, tiled=True)
    return contract(sink_rows, source_full, perambulators)


def solution(mesh):
    placed = (
        P(("cfg", "tm"), ("space", "spin"), None, None),
        P(),
        P(("cfg", "tm"), None),
        P(),
        P(("cfg", "tm"), None, None),
    )
    return jax.shard_map(
        per_device,
        mesh=mesh,
        in_specs=placed,
        out_specs=P(("cfg", "tm"), None, ("space", "spin"), None, None),
        check_vma=False,
    )
```

profile of v0, /device:TPU:0, one launch (start us, length us, event | category | flops | bytes accessed | tf_op | source)
XLA Modules:
  0.0 155.7 jit_solution(13972722888859161238)
XLA Ops:
  6.5 77.3 %while.13 = (s32[]{:T(128)}, f32[2,8,64,128]{3,2,1,0:T(8,128)}, bf16[2,512,3,128]{3,1,2,0:T(8,128)(2,1)}, s32[8,3]{0,1:T(4,128)}, s32[]{:T(128)}, /*index=5*/s32[]{:T(128)}) while((s32[]{:T(128)}, f32[2,8,64,128]{3,2,1,0:T(8,128)}, bf16[2,512,3,128]{3,1,2,0:T(8,128)(2,1)}, s32[8,3]{0,1:T(4,128)}, s32[]{:T(128)}, /*index=5*/s32[]{:T(128)}) %tuple.147), condition=%wide.region_1.2_spmd, body=%wide.region_0.1_spmd.sunk | while | flops 427274240 | bytes 61539204 | solution.py:85
  9.8 2.0 %fusion.177 = (f32[512]{0:T(512)S(1)}, f32[512]{0:T(512)S(1)}) fusion(s32[]{:T(128)} %bitcast.241, s32[]{:T(128)} %bitcast.242, s32[]{:T(128)} %get-tuple-element.440, s32[]{:T(128)} %bitcast.243), kind=kLoop, calls=%fused_computation.193.clone.1 | loop fusion | flops 30208 | bytes 4112 | tf_op jit(solution)/shard_map/while/body/eval_jaxpr/sin | solution.py:32
  12.0 1.9 %fusion.178 = (f32[512]{0:T(512)S(1)}, f32[512]{0:T(512)S(1)}) fusion(s32[]{:T(128)} %bitcast.245, s32[]{:T(128)} %bitcast.246, s32[]{:T(128)} %get-tuple-element.440, s32[]{:T(128)} %bitcast.247), kind=kLoop, calls=%fused_computation.195.clone.1 | loop fusion | flops 30208 | bytes 4112 | tf_op jit(solution)/shard_map/while/body/eval_jaxpr/sin | solution.py:32
  14.3 1.1 copy.82
  18.7 1.9 %fusion.182 = (f32[512]{0:T(512)S(1)}, f32[512]{0:T(512)S(1)}) fusion(s32[]{:T(128)} %bitcast.250, s32[]{:T(128)} %bitcast.251, s32[]{:T(128)} %get-tuple-element.440, s32[]{:T(128)} %bitcast.252), kind=kLoop, calls=%fused_computation.189.clone.1 | loop fusion | flops 30208 | bytes 4112 | tf_op jit(solution)/shard_map/while/body/eval_jaxpr/sin | solution.py:32
  20.7 1.9 %fusion.183 = (f32[512]{0:T(512)S(1)}, f32[512]{0:T(512)S(1)}) fusion(s32[]{:T(128)} %bitcast.253, s32[]{:T(128)} %bitcast.254, s32[]{:T(128)} %get-tuple-element.440, s32[]{:T(128)} %bitcast.255), kind=kLoop, calls=%fused_computation.191.clone.1 | loop fusion | flops 30208 | bytes 4112 | tf_op jit(solution)/shard_map/while/body/eval_jaxpr/sin | solution.py:32
  27.5 1.9 %fusion.187 = (f32[512]{0:T(512)S(1)}, f32[512]{0:T(512)S(1)}) fusion(s32[]{:T(128)} %bitcast.258, s32[]{:T(128)} %bitcast.259, s32[]{:T(128)} %get-tuple-element.440, s32[]{:T(128)} %bitcast.260), kind=kLoop, calls=%fused_computation.185.clone.1 | loop fusion | flops 30208 | bytes 4112 | tf_op jit(solution)/shard_map/while/body/eval_jaxpr/sin | solution.py:32
  29.4 2.0 %fusion.188 = (f32[512]{0:T(512)S(1)}, f32[512]{0:T(512)S(1)}) fusion(s32[]{:T(128)} %bitcast.261, s32[]{:T(128)} %bitcast.262, s32[]{:T(128)} %get-tuple-element.440, s32[]{:T(128)} %bitcast.263), kind=kLoop, calls=%fused_computation.187.clone.1 | loop fusion | flops 30208 | bytes 4112 | tf_op jit(solution)/shard_map/while/body/eval_jaxpr/sin | solution.py:32
  36.2 1.9 %fusion.192 = (f32[512]{0:T(512)S(1)}, f32[512]{0:T(512)S(1)}) fusion(s32[]{:T(128)} %bitcast.266, s32[]{:T(128)} %bitcast.267, s32[]{:T(128)} %get-tuple-element.440, s32[]{:T(128)} %bitcast.268), kind=kLoop, calls=%fused_computation.181.clone.1 | loop fusion | flops 30208 | bytes 4112 | tf_op jit(solution)/shard_map/while/body/eval_jaxpr/sin | solution.py:32
  38.2 1.9 %fusion.193 = (f32[512]{0:T(512)S(1)}, f32[512]{0:T(512)S(1)}) fusion(s32[]{:T(128)} %bitcast.269, s32[]{:T(128)} %bitcast.270, s32[]{:T(128)} %get-tuple-element.440, s32[]{:T(128)} %bitcast.271), kind=kLoop, calls=%fused_computation.183.clone.1 | loop fusion | flops 30208 | bytes 4112 | tf_op jit(solution)/shard_map/while/body/eval_jaxpr/sin | solution.py:32
  48.4 2.0 %fusion.177 = (f32[512]{0:T(512)S(1)}, f32[512]{0:T(512)S(1)}) fusion(s32[]{:T(128)} %bitcast.241, s32[]{:T(128)} %bitcast.242, s32[]{:T(128)} %get-tuple-element.440, s32[]{:T(128)} %bitcast.243), kind=kLoop, calls=%fused_computation.193.clone.1 | loop fusion | flops 30208 | bytes 4112 | tf_op jit(solution)/shard_map/while/body/eval_jaxpr/sin | solution.py:32
  50.6 1.9 %fusion.178 = (f32[512]{0:T(512)S(1)}, f32[512]{0:T(512)S(1)}) fusion(s32[]{:T(128)} %bitcast.245, s32[]{:T(128)} %bitcast.246, s32[]{:T(128)} %get-tuple-element.440, s32[]{:T(128)} %bitcast.247), kind=kLoop, calls=%fused_computation.195.clone.1 | loop fusion | flops 30208 | bytes 4112 | tf_op jit(solution)/shard_map/while/body/eval_jaxpr/sin | solution.py:32
  57.4 1.9 %fusion.182 = (f32[512]{0:T(512)S(1)}, f32[512]{0:T(512)S(1)}) fusion(s32[]{:T(128)} %bitcast.250, s32[]{:T(128)} %bitcast.251, s32[]{:T(128)} %get-tuple-element.440, s32[]{:T(128)} %bitcast.252), kind=kLoop, calls=%fused_computation.189.clone.1 | loop fusion | flops 30208 | bytes 4112 | tf_op jit(solution)/shard_map/while/body/eval_jaxpr/sin | solution.py:32
  59.3 1.9 %fusion.183 = (f32[512]{0:T(512)S(1)}, f32[512]{0:T(512)S(1)}) fusion(s32[]{:T(128)} %bitcast.253, s32[]{:T(128)} %bitcast.254, s32[]{:T(128)} %get-tuple-element.440, s32[]{:T(128)} %bitcast.255), kind=kLoop, calls=%fused_computation.191.clone.1 | loop fusion | flops 30208 | bytes 4112 | tf_op jit(solution)/shard_map/while/body/eval_jaxpr/sin | solution.py:32
  66.1 1.9 %fusion.187 = (f32[512]{0:T(512)S(1)}, f32[512]{0:T(512)S(1)}) fusion(s32[]{:T(128)} %bitcast.258, s32[]{:T(128)} %bitcast.259, s32[]{:T(128)} %get-tuple-element.440, s32[]{:T(128)} %bitcast.260), kind=kLoop, calls=%fused_computation.185.clone.1 | loop fusion | flops 30208 | bytes 4112 | tf_op jit(solution)/shard_map/while/body/eval_jaxpr/sin | solution.py:32
  68.0 2.0 %fusion.188 = (f32[512]{0:T(512)S(1)}, f32[512]{0:T(512)S(1)}) fusion(s32[]{:T(128)} %bitcast.261, s32[]{:T(128)} %bitcast.262, s32[]{:T(128)} %get-tuple-element.440, s32[]{:T(128)} %bitcast.263), kind=kLoop, calls=%fused_computation.187.clone.1 | loop fusion | flops 30208 | bytes 4112 | tf_op jit(solution)/shard_map/while/body/eval_jaxpr/sin | solution.py:32
  74.9 1.9 %fusion.192 = (f32[512]{0:T(512)S(1)}, f32[512]{0:T(512)S(1)}) fusion(s32[]{:T(128)} %bitcast.266, s32[]{:T(128)} %bitcast.267, s32[]{:T(128)} %get-tuple-element.440, s32[]{:T(128)} %bitcast.268), kind=kLoop, calls=%fused_computation.181.clone.1 | loop fusion | flops 30208 | bytes 4112 | tf_op jit(solution)/shard_map/while/body/eval_jaxpr/sin | solution.py:32
  76.8 1.9 %fusion.193 = (f32[512]{0:T(512)S(1)}, f32[512]{0:T(512)S(1)}) fusion(s32[]{:T(128)} %bitcast.269, s32[]{:T(128)} %bitcast.270, s32[]{:T(128)} %get-tuple-element.440, s32[]{:T(128)} %bitcast.271), kind=kLoop, calls=%fused_computation.183.clone.1 | loop fusion | flops 30208 | bytes 4112 | tf_op jit(solution)/shard_map/while/body/eval_jaxpr/sin | solution.py:32
  83.9 4.4 %reshape.323 = bf16[4,64,16,2,64]{4,3,2,1,0:T(2,128)(2,1)S(1)} reshape(bf16[4,64,2048]{2,1,0:T(8,128)(2,1)} %param.11) | data formatting | bytes 2097152 | tf_op jit(solution)/shard_map/reshape | solution.py:53
  88.3 4.8 %slice_negate_fusion = (bf16[4,64,16,1,64]{4,3,2,1,0:T(2,128)(2,1)S(1)}, bf16[4,64,16,1,64]{4,3,2,1,0:T(2,128)(2,1)S(1)}) fusion(bf16[4,64,16,2,64]{4,3,2,1,0:T(2,128)(2,1)S(1)} %reshape.323), kind=kLoop, calls=%fused_computation.201 | loop fusion | flops 262144 | bytes 2097152 | tf_op jit(solution)/shard_map/neg | solution.py:54
  93.2 5.6 %pad_maximum_fusion.8 = bf16[4,64,16,2,64]{4,3,2,1,0:T(2,128)(2,1)S(1)} fusion(bf16[4,64,16,1,64]{4,3,2,1,0:T(2,128)(2,1)S(1)} %get-tuple-element.226, bf16[4,64,16,1,64]{4,3,2,1,0:T(2,128)(2,1)S(1)} %get-tuple-element.225), kind=kLoop, calls=%fused_computation.202 | loop fusion | flops 2097152 | bytes 2097152 | tf_op jit(solution)/shard_map/stack | solution.py:54
  98.8 2.5 %reshape.324 = bf16[4,64,2048]{2,1,0:T(8,128)(2,1)} reshape(bf16[4,64,16,2,64]{4,3,2,1,0:T(2,128)(2,1)S(1)} %pad_maximum_fusion.8) | data formatting | bytes 2097152 | tf_op jit(solution)/shard_map/reshape | solution.py:54
  102.6 5.8 %reduce-scatter.2.cloned.1.call-done = f32[2,8,16,128]{3,2,1,0:T(8,128)} async-done(((f32[2,8,64,128]{3,2,1,0:T(8,128)}), f32[2,8,16,128]{3,2,1,0:T(8,128)}) %reduce-scatter.2.cloned.1.call-update) | async-done | bytes 131088 | tf_op jit(solution)/shard_map/reduce_scatter | solution.py:90
  109.3 13.9 %all_gather.6 = bf16[8,8,16,128]{3,2,1,0:T(8,128)(2,1)S(1)} all-gather(bf16[2,8,16,128]{3,2,1,0:T(8,128)(2,1)S(1)} %convert_element_type.279), channel_id=1, replica_groups=mesh['cfg'=2,'tm'=4,'space'=2,'spin'=2] {'tm'}, dimensions={0}, use_global_device_ids=true | all-gather | bytes 327680 | tf_op jit(solution)/shard_map/all_gather | solution.py:97
  123.5 2.0 %convolution_convert_fusion.2 = bf16[4,128,2048]{2,1,0:T(8,128)(2,1)} fusion(bf16[4,64,2048]{2,1,0:T(8,128)(2,1)S(1)} %copy-done.4, bf16[4,64,2048]{2,1,0:T(8,128)(2,1)S(1)} %copy-done.3, bf16[1,4,128,128]{3,1,2,0:T(4,128)(2,1)S(1)} %fusion.88), kind=kOutput, calls=%fused_computation.200 | convolution fusion | flops 273678336 | bytes 4325376 | tf_op jit(solution)/shard_map/kmx,kxc->kmc/dot_general | solution.py:59
  125.6 2.9 %reshape.325 = bf16[4,8,256,128]{3,2,1,0:T(8,128)(2,1)S(1)} reshape(bf16[4,128,2048]{2,1,0:T(8,128)(2,1)} %convolution_convert_fusion.2) | data formatting | bytes 4194304 | tf_op jit(solution)/shard_map/reshape | solution.py:62
  128.8 7.0 %all_gather.7 = bf16[4,8,64,128]{3,2,1,0:T(8,128)(2,1)} all-gather(bf16[4,8,16,128]{3,2,1,0:T(8,128)(2,1)S(1)} %bitcast.290), channel_id=1, replica_groups=mesh['cfg'=2,'tm'=4,'space'=2,'spin'=2] {'space','spin'}, dimensions={2}, use_global_device_ids=true | all-gather | bytes 655360 | tf_op jit(solution)/shard_map/all_gather | solution.py:109
  135.7 2.4 %reshape.327 = bf16[4,8,64,2,64]{4,3,2,1,0:T(2,128)(2,1)S(1)} reshape(bf16[4,8,64,128]{3,2,1,0:T(8,128)(2,1)} %all_gather.7) | data formatting | bytes 1048576 | tf_op jit(solution)/shard_map/reshape | solution.py:63
  138.2 2.3 %slice_negate_fusion.1 = (bf16[4,8,64,1,64]{4,3,2,1,0:T(2,128)(2,1)S(1)}, bf16[4,8,64,1,64]{4,3,2,1,0:T(2,128)(2,1)S(1)}) fusion(bf16[4,8,64,2,64]{4,3,2,1,0:T(2,128)(2,1)S(1)} %reshape.327), kind=kLoop, calls=%fused_computation.209 | loop fusion | flops 131072 | bytes 1048576 | tf_op jit(solution)/shard_map/neg | solution.py:64
  140.6 3.6 %pad_maximum_fusion.9 = bf16[4,8,64,2,64]{4,3,2,1,0:T(2,128)(2,1)} fusion(bf16[4,8,64,1,64]{4,3,2,1,0:T(2,128)(2,1)S(1)} %get-tuple-element.228, bf16[4,8,64,1,64]{4,3,2,1,0:T(2,128)(2,1)S(1)} %get-tuple-element.227), kind=kLoop, calls=%fused_computation.210 | loop fusion | flops 1048576 | bytes 1048576 | tf_op jit(solution)/shard_map/stack | solution.py:64
  144.1 2.4 %stack_reshape.3 = bf16[4,8,1,64,128]{4,3,1,0,2:T(8,128)(2,1)S(1)} reshape(bf16[4,8,64,2,64]{4,3,2,1,0:T(2,128)(2,1)} %pad_maximum_fusion.9) | data formatting | bytes 1048576 | tf_op jit(solution)/shard_map/stack;reshape | solution.py:67
  146.8 2.0 %convolution_convert_fusion.3 = bf16[4,8,256,128]{3,2,1,0:T(8,128)(2,1)} fusion(bf16[4,8,256,128]{3,2,1,0:T(8,128)(2,1)S(1)} %reshape.325, bf16[4,8,128,128]{3,2,1,0:T(8,128)(2,1)S(1)} %bitcast.287), kind=kOutput, calls=%fused_computation.206 | convolution fusion | flops 269484032 | bytes 5242880 | tf_op jit(solution)/shard_map/kpmx,kpnx->kpmn/dot_general | solution.py:68
  (124 shorter events, 47.5 us)
Async XLA Ops:
  6.5 94.8 %copy-start = (s32[8]{0:T(128)S(1)}, s32[8]{0:T(128)}, u32[]{:S(2)}) copy-start(s32[8]{0:T(128)} %param.10) | copy-start | bytes 100
  6.5 101.8 %reduce-scatter.2.cloned.1.call-start = ((), (), s32[]{:S(2)}) async-start(), calls=%async_computation.1 | async-start | bytes 655360 | tf_op jit(solution)/shard_map/reduce_scatter | solution.py:90
  6.5 1.9 %copy-start.5 = (s32[8,3]{0,1:T(4,128)S(1)}, s32[8,3]{0,1:T(4,128)}, u32[]{:S(2)}) copy-start(s32[8,3]{0,1:T(4,128)} %get-tuple-element.439) | copy-start | bytes 292 | tf_op jit(solution)/shard_map/while
  42.7 1.3 copy-start.1
  42.7 1.6 %copy-start.6 = (f32[2,8,64,128]{3,2,1,0:T(8,128)S(1)}, f32[2,8,64,128]{3,2,1,0:T(8,128)}, u32[]{:S(2)}) copy-start(f32[2,8,64,128]{3,2,1,0:T(8,128)} %get-tuple-element.431) | copy-start | bytes 1572868 | tf_op jit(solution)/shard_map/while
  44.4 0.8 copy-start.7
  45.2 1.9 %copy-start.5 = (s32[8,3]{0,1:T(4,128)S(1)}, s32[8,3]{0,1:T(4,128)}, u32[]{:S(2)}) copy-start(s32[8,3]{0,1:T(4,128)} %get-tuple-element.439) | copy-start | bytes 292 | tf_op jit(solution)/shard_map/while
  81.3 1.3 copy-start.1
  81.4 1.6 %copy-start.6 = (f32[2,8,64,128]{3,2,1,0:T(8,128)S(1)}, f32[2,8,64,128]{3,2,1,0:T(8,128)}, u32[]{:S(2)}) copy-start(f32[2,8,64,128]{3,2,1,0:T(8,128)} %get-tuple-element.431) | copy-start | bytes 1572868 | tf_op jit(solution)/shard_map/while
  83.0 0.8 copy-start.7
  98.8 2.5 %copy-start.8 = (s32[4,2]{0,1:T(2,128)S(1)}, s32[4,2]{0,1:T(2,128)}, u32[]{:S(2)}) copy-start(s32[4,2]{0,1:T(2,128)} %param.9) | copy-start | bytes 100
  98.8 24.7 %copy-start.3 = (bf16[4,64,2048]{2,1,0:T(8,128)(2,1)S(1)}, bf16[4,64,2048]{2,1,0:T(8,128)(2,1)}, u32[]{:S(2)}) copy-start(bf16[4,64,2048]{2,1,0:T(8,128)(2,1)} %param.11) | copy-start | bytes 3145732
  101.3 22.3 %copy-start.4 = (bf16[4,64,2048]{2,1,0:T(8,128)(2,1)S(1)}, bf16[4,64,2048]{2,1,0:T(8,128)(2,1)}, u32[]{:S(2)}) copy-start(bf16[4,64,2048]{2,1,0:T(8,128)(2,1)} %reshape.324) | copy-start | bytes 3145732
  140.5 6.0 %copy-start.2 = (bf16[4,8,64,128]{3,2,1,0:T(8,128)(2,1)S(1)}, bf16[4,8,64,128]{3,2,1,0:T(8,128)(2,1)}, u32[]{:S(2)}) copy-start(bf16[4,8,64,128]{3,2,1,0:T(8,128)(2,1)} %all_gather.7) | copy-start | bytes 1572868
Sparse Core Ops, SparseCore 0:
  84.0 24.3 reduce-scatter.1
where the time goes:
time: 156 us
  other arithmetic  52.9 us (34%)
  local copies, waits for them, and re-layouts  42.6 us (27%)
  blocking collectives  20.9 us (13%)
  matrix products  19.3 us (12%)
  between operations  13.6 us (9%)
  waiting for transfers between devices  5.81 us (4%)
    sin x16, other arithmetic, elemental(): sines = jnp.sin(angles)[:, None, None]  31 us
    another operation x16, local copies, waits for them, and re-layouts, elemental(): jnp.stack([upper_rows, lower_rows], axis=2)  18 us
    dot_general x16, matrix products, elemental(): lax.dot_general(conj_left, phased, (((0,), (0,)), ((), ())), preferred_el...  14.7 us
    all_gather x1, blocking collectives, per_device(): lax.all_gather(part, 'tm', axis=0, tiled=True)  13.9 us
    all_gather x1, blocking collectives, per_device(): lax.all_gather(source_share, ('space', 'spin'), axis=2, tiled=True)  6.98 us
    reduce_scatter x1, waiting for transfers between devices, per_device(): lax.psum_scatter(partial_value, ('space', 'spin'), scatter_dimension=2, t...  5.8 us
    another operation x1, other arithmetic, contract(): jnp.stack([-parts[:, :, :, 1], parts[:, :, :, 0]], axis=3)  5.6 us
    neg x1, other arithmetic, contract(): -parts[:, :, :, 1]  4.85 us
  transfers between devices with their start and end apart: 1, of which 1 were waited for; matrix products, arithmetic and copies ran while one was open for 12% of the time, Pallas kernels for 0%

commit v1 on v0

v1 whole, which is shorter than its diff:
```python
import functools

import jax
import jax.numpy as jnp
from jax import lax
from jax.experimental import pallas as pl
from jax.experimental.pallas import tpu as pltpu
from jax.sharding import PartitionSpec as P

LAT = 32
TURN = 6.283185307179586
BF16 = jnp.bfloat16
F32 = jnp.float32
MESH = pl.DeviceIdType.MESH


def phase_tables(momenta, first_site, site_count, moms):
    shape = (site_count, 128)
    lane = lax.broadcasted_iota(jnp.int32, (1, 128), 1)
    rows = []
    for axis in range(3):
        row = jnp.zeros((1, 128), jnp.int32)
        for m in range(moms):
            row = jnp.where(lane == m, momenta[axis, m], row)
        rows.append(row)
    site = first_site + lax.broadcasted_iota(jnp.int32, shape, 0)
    coord_x = lax.rem(site, LAT)
    coord_y = lax.rem(lax.div(site, LAT), LAT)
    coord_z = lax.div(site, LAT * LAT)
    wavenum = (rows[0] * coord_x + rows[1] * coord_y + rows[2] * coord_z) & (LAT - 1)
    quadrant = (wavenum + LAT // 8) >> 3
    x = (wavenum - quadrant * (LAT // 4)).astype(F32) * (TURN / LAT)
    y = x * x
    sin = x * (1 + y * (-1 / 6 + y * (1 / 120 + y * (-1 / 5040 + y * (1 / 362880)))))
    cos = 1 + y * (-1 / 2 + y * (1 / 24 + y * (-1 / 720 + y * (1 / 40320 + y * (-1 / 3628800)))))
    odd = (quadrant & 1) == 1
    cos_all = jnp.where(odd, sin, cos)
    sin_all = jnp.where(odd, cos, sin)
    cos_all = jnp.where(((quadrant + 1) & 2) == 2, -cos_all, cos_all)
    sin_all = jnp.where((quadrant & 2) == 2, -sin_all, sin_all)
    return cos_all, sin_all


def kernel(
    dims, eig, momenta, pairs, slots, tau, out,
    cos_tab, sin_tab, turned, part, arrived, sinks, sources, right, half,
    rs_send, rs_recv, z_send, z_recv, own_send, own_recv, core_send, core_recv, fwd_send, fwd_recv,
    *gathered,
):
    n_t, n_x, n_p, chunks, site_count, colours = dims
    group = n_x * n_p
    slices = eig.shape[0]
    moms = momenta.shape[1]
    pair_count, vectors = tau.shape[0], tau.shape[1]
    width = 2 * vectors
    spins = tau.shape[2] // width
    per = moms // chunks
    share = vectors // group
    rows = per * share
    t, sx, sp = lax.axis_index("tm"), lax.axis_index("space"), lax.axis_index("spin")
    pos = sx * n_p + sp

    lane = lax.broadcasted_iota(jnp.int32, (1, width), 1)
    minus_first = jnp.where(lane < vectors, -1.0, 1.0).astype(F32)

    def swap(block):
        return pltpu.roll(block, vectors, 1)

    def peer(d):
        other = lax.rem(pos + d, group)
        return other, {"space": lax.div(other, n_p), "spin": lax.rem(other, n_p)}

    cos_value, sin_value = phase_tables(momenta, pos * site_count, site_count, moms)
    cos_tab[...] = cos_value
    sin_tab[...] = sin_value

    step = 16

    def compute(ch):
        def block(i, carry):
            s0 = pl.multiple_of(i * step, step)
            c_rows = cos_tab[pl.ds(s0, step), :]
            s_rows = sin_tab[pl.ds(s0, step), :]
            values = []
            for r in range(slices):
                for c in range(colours):
                    v = eig[r, pl.ds(c * site_count + s0, step), :].astype(F32)
                    values.append((r, c, v, swap(v) * minus_first))
            for mi in range(per):
                m = ch * per + mi
                cb = jnp.broadcast_to(c_rows[:, m : m + 1], (step, width))
                sb = jnp.broadcast_to(s_rows[:, m : m + 1], (step, width))
                for r, c, v, j in values:
                    turned[r, pl.ds(c * site_count + s0, step), mi * width : (mi + 1) * width] = (
                        cb * v + sb * j
                    ).astype(BF16)
            return carry

        lax.fori_loop(0, site_count // step, block, 0)
        for r in range(slices):
            product = lax.dot_general(
                eig[r], turned[r], (((0,), (0,)), ((), ())), preferred_element_type=F32
            )
            for mi in range(per):
                top = product[:vectors, mi * width : (mi + 1) * width]
                low = product[vectors:, mi * width : (mi + 1) * width]
                value = (top - swap(low) * minus_first).astype(BF16)
                for g in range(group):
                    part[ch, g, pl.ds(r * rows + mi * share, share), :] = value[g * share : (g + 1) * share]

    def rs_copies(ch):
        copies = []
        for d in range(1, group):
            other, where = peer(d)
            copies.append(pltpu.make_async_remote_copy(
                src_ref=part.at[ch, other], dst_ref=arrived.at[ch, d - 1],
                send_sem=rs_send.at[ch, d - 1], recv_sem=rs_recv.at[ch, d - 1],
                device_id=where, device_id_type=MESH))
        return copies

    def z_copies(ch):
        own = gathered[ch].at[pl.ds(t * slices, slices)]
        return [
            pltpu.make_async_remote_copy(
                src_ref=own, dst_ref=own,
                send_sem=z_send.at[ch, d - 1], recv_sem=z_recv.at[ch, d - 1],
                device_id={"tm": lax.rem(t + d, n_t)}, device_id_type=MESH)
            for d in range(1, n_t)
        ]

    def own_copies(ch):
        own = sources.at[ch, pos]
        across = [
            pltpu.make_async_remote_copy(
                src_ref=own, dst_ref=own,
                send_sem=own_send.at[ch, d - 1], recv_sem=own_recv.at[ch, d - 1],
                device_id={"space": lax.rem(sx + d, n_x)}, device_id_type=MESH)
            for d in range(1, n_x)
        ]
        core = [
            pltpu.make_async_remote_copy(
                src_ref=own, dst_ref=own,
                send_sem=core_send.at[ch, e - 1], recv_sem=core_recv.at[ch, e - 1],
                device_id={"spin": lax.rem(sp + e, n_p)}, device_id_type=MESH)
            for e in range(1, n_p)
        ]
        return across, core

    def forward_copies(ch, d):
        from_pos = lax.rem(sx + n_x - d, n_x) * n_p + sp
        block = sources.at[ch, from_pos]
        return [
            pltpu.make_async_remote_copy(
                src_ref=block, dst_ref=block,
                send_sem=fwd_send.at[ch, d - 1, e - 1], recv_sem=fwd_recv.at[ch, d - 1, e - 1],
                device_id={"spin": lax.rem(sp + e, n_p)}, device_id_type=MESH)
            for e in range(1, n_p)
        ]

    def reduce_share(ch):
        total = part[ch, pos].astype(F32)
        for d in range(1, group):
            total = total + arrived[ch, d - 1].astype(F32)
        gathered[ch][pl.ds(t * slices, slices)] = total.astype(BF16).reshape(slices, rows, width)

    def select(ch):
        for k in range(pair_count):
            sinks[ch, k] = gathered[ch][slots[pairs[0, k]]]
            sources[ch, pos, k] = gathered[ch][slots[pairs[1, k]]]

    def prepare(k, carry):
        right[k, :vectors, :] = tau[k]
        for g in range(spins):
            block = tau[k, :, g * width : (g + 1) * width].astype(F32)
            right[k, vectors:, g * width : (g + 1) * width] = (swap(block) * minus_first).astype(BF16)
        return carry

    def contract(ch):
        def pair(k, carry):
            halfway = jnp.dot(sinks[ch, k], right[k], preferred_element_type=F32)
            for g in range(spins):
                half[pl.ds(g, rows, stride=spins), :] = halfway[:, g * width : (g + 1) * width]
            for mi in range(per):
                q = jnp.concatenate(
                    [sources[ch, g, k, mi * share : (mi + 1) * share, :] for g in range(group)], axis=0)
                swapped = (swap(q.astype(F32)) * minus_first).astype(BF16)
                conjugate = jnp.concatenate([q, swapped], axis=0)
                left = half[mi * share * spins : (mi + 1) * share * spins, :].astype(BF16)
                loops = lax.dot_general(
                    left, conjugate, (((1,), (1,)), ((), ())), preferred_element_type=F32)
                out[k, ch * per + mi] = loops.astype(BF16)
            return carry

        lax.fori_loop(0, pair_count, pair, 0)

    rs, zs, owns, fwds = {}, {}, {}, {}
    barrier = pltpu.get_barrier_semaphore()
    for d in range(1, group):
        pl.semaphore_signal(barrier, inc=1, device_id=peer(d)[1], device_id_type=MESH)
    for d in range(1, n_t):
        pl.semaphore_signal(barrier, inc=1, device_id={"tm": lax.rem(t + d, n_t)}, device_id_type=MESH)
    for ch in range(chunks):
        compute(ch)
        if ch == 0:
            pl.semaphore_wait(barrier, group - 1 + n_t - 1)
        rs[ch] = rs_copies(ch)
        for copy in rs[ch]:
            copy.start()
        if ch >= 1:
            for copy in rs[ch - 1]:
                copy.wait_recv()
            reduce_share(ch - 1)
            zs[ch - 1] = z_copies(ch - 1)
            for copy in zs[ch - 1]:
                copy.start()
    lax.fori_loop(0, pair_count, prepare, 0)
    last = chunks - 1
    for copy in rs[last]:
        copy.wait_recv()
    reduce_share(last)
    zs[last] = z_copies(last)
    for copy in zs[last]:
        copy.start()
    for ch in range(chunks):
        for copy in zs[ch]:
            copy.wait_recv()
        select(ch)
        owns[ch] = own_copies(ch)
        for copy in owns[ch][0] + owns[ch][1]:
            copy.start()
    for ch in range(chunks):
        fwds[ch] = []
        for d in range(1, n_x):
            owns[ch][0][d - 1].wait_recv()
            fwds[ch].append(forward_copies(ch, d))
            for copy in fwds[ch][-1]:
                copy.start()
    for ch in range(chunks):
        for copy in owns[ch][1]:
            copy.wait_recv()
        for group_copies in fwds[ch]:
            for copy in group_copies:
                copy.wait_recv()
        contract(ch)
    for ch in range(chunks):
        for copy in rs[ch] + zs[ch] + owns[ch][0] + owns[ch][1]:
            copy.wait_send()
        for group_copies in fwds[ch]:
            for copy in group_copies:
                copy.wait_send()


CHUNKS = 2


def per_device(eigenvectors, momenta, time_pairs, slot_map, perambulators):
    n_t, n_x, n_p = lax.axis_size("tm"), lax.axis_size("space"), lax.axis_size("spin")
    group = n_x * n_p
    slices, site_count, colours, width = eigenvectors.shape
    moms = momenta.shape[0]
    pair_count, vectors, columns = perambulators.shape
    spins = columns // width
    share = vectors // group
    per = moms // CHUNKS
    rows = per * share
    eig = jnp.transpose(eigenvectors, (0, 2, 1, 3)).reshape(slices, colours * site_count, width)
    vmem = pl.BlockSpec(memory_space=pltpu.VMEM)
    smem = pl.BlockSpec(memory_space=pltpu.SMEM)
    dma = pltpu.SemaphoreType.DMA
    out = pl.pallas_call(
        functools.partial(kernel, (n_t, n_x, n_p, CHUNKS, site_count, colours)),
        out_shape=jax.ShapeDtypeStruct((pair_count, moms, share * spins, width), BF16),
        in_specs=[vmem, smem, smem, smem, vmem],
        out_specs=vmem,
        scratch_shapes=[
            pltpu.VMEM((site_count, 128), F32),
            pltpu.VMEM((site_count, 128), F32),
            pltpu.VMEM((slices, colours * site_count, per * width), BF16),
            pltpu.VMEM((CHUNKS, group, slices * rows, width), BF16),
            pltpu.VMEM((CHUNKS, group - 1, slices * rows, width), BF16),
            pltpu.VMEM((CHUNKS, pair_count, rows, width), BF16),
            pltpu.VMEM((CHUNKS, group, pair_count, rows, width), BF16),
            pltpu.VMEM((pair_count, width, columns), BF16),
            pltpu.VMEM((rows * spins, width), F32),
            dma((CHUNKS, group - 1)), dma((CHUNKS, group - 1)),
            dma((CHUNKS, n_t - 1)), dma((CHUNKS, n_t - 1)),
            dma((CHUNKS, n_x - 1)), dma((CHUNKS, n_x - 1)),
            dma((CHUNKS, n_p - 1)), dma((CHUNKS, n_p - 1)),
            dma((CHUNKS, n_x - 1, n_p - 1)), dma((CHUNKS, n_x - 1, n_p - 1)),
        ] + [pltpu.VMEM((n_t * slices, rows, width), BF16)] * CHUNKS,
        compiler_params=pltpu.CompilerParams(
            collective_id=0, has_side_effects=True, vmem_limit_bytes=40 * 1024 * 1024),
    )(eig, momenta.T, time_pairs.T, slot_map, perambulators)
    return out.reshape(pair_count, moms, share, spins, width)


def solution(mesh):
    placed = (
        P(("cfg", "tm"), ("space", "spin"), None, None),
        P(),
        P(("cfg", "tm"), None),
        P(),
        P(("cfg", "tm"), None, None),
    )
    return jax.shard_map(
        per_device,
        mesh=mesh,
        in_specs=placed,
        out_specs=P(("cfg", "tm"), None, ("space", "spin"), None, None),
        check_vma=False,
    )
```

time: 156 us -> 33.3 us (0.21)
  other arithmetic: 52.9 us -> 0 us
  local copies, waits for them, and re-layouts: 42.6 us -> 5.69 us
  Pallas kernels: 0 us -> 27.3 us
  blocking collectives: 20.9 us -> 0 us
  matrix products: 19.3 us -> 0 us
  between operations: 13.6 us -> 0.01 us
  waiting for transfers between devices: 5.81 us -> 0 us
    sin x16 -> x0, other arithmetic: 31 us -> none  [elemental(): sines = jnp.sin(angles)[:, None, None]]
    pallas_call x0 -> x1, Pallas kernels: none -> 27.3 us  [per_device(): pl.pallas_call(functools.partial(kernel, (n_t, n_x, n_p, CHUNKS, site_cou...]
    all_gather x2 -> x0, blocking collectives: 20.9 us -> none  [the longest x1 13.9 us: per_device(): lax.all_gather(part, 'tm', axis=0, tiled=True)]
    another operation x18 -> x0, local copies, waits for them, and re-layouts: 20.5 us -> none  [the longest x16 18 us: elemental(): jnp.stack([upper_rows, lower_rows], axis=2)]
    dot_general x20 -> x0, matrix products: 19.3 us -> none  [the longest x16 14.7 us: elemental(): lax.dot_general(conj_left, phased, (((0,), (0,)), ((), ())), preferred_el...]
    another operation x43 -> x0, other arithmetic: 13.7 us -> none  [the longest x1 5.6 us: contract(): jnp.stack([-parts[:, :, :, 1], parts[:, :, :, 0]], axis=3)]
    reshape x6 -> x0, local copies, waits for them, and re-layouts: 13.2 us -> none  [the longest x1 4.43 us: contract(): parts = perambulators.reshape(pair_count, vectors, 16, 2, vectors)]
    neg x2 -> x0, other arithmetic: 7.19 us -> none  [the longest x1 4.85 us: contract(): -parts[:, :, :, 1]]
  transfers between devices with their start and end apart: 1 -> 0, of which waited for: 1 -> 0; matrix products, arithmetic and copies ran while one was open for 12% -> 0% of each run, Pallas kernels for 0% -> 0%
where the time goes in v1:
time: 33.3 us; the launch traced here: 33 us
  Pallas kernels  27.3 us (82%)
  local copies, waits for them, and re-layouts  5.69 us (17%)
    pallas_call x1, Pallas kernels, per_device(): pl.pallas_call(functools.partial(kernel, (n_t, n_x, n_p, CHUNKS, site_cou...  27.3 us
    unnamed x11, local copies, waits for them, and re-layouts  5.69 us

profile of v1, /device:TPU:0, one launch (start us, length us, event | category | flops | bytes accessed | tf_op | source)
XLA Modules:
  0.0 33.0 jit_solution(1939602826175772239)
XLA Ops:
  0.0 0.0 copy-start
  0.0 1.2 %copy-done = bf16[4,64,2048]{2,1,0:T(8,128)(2,1)S(1)} copy-done((bf16[4,64,2048]{2,1,0:T(8,128)(2,1)S(1)}, bf16[4,64,2048]{2,1,0:T(8,128)(2,1)}, u32[]{:S(2)}) %copy-start) | copy-done | bytes 1048600
  1.2 0.0 copy-start.1
  1.2 1.1 %copy-done.1 = bf16[2,512,3,128]{3,1,2,0:T(8,128)(2,1)S(1)} copy-done((bf16[2,512,3,128]{3,1,2,0:T(8,128)(2,1)S(1)}, bf16[2,512,3,128]{3,1,2,0:T(8,128)(2,1)}, u32[]{:S(2)}) %copy-start.1) | copy-done | bytes 786456
  2.4 0.0 copy-start.2
  2.4 0.7 %copy-done.2 = s32[8,3]{0,1:T(4,128)S(1)} copy-done((s32[8,3]{0,1:T(4,128)S(1)}, s32[8,3]{0,1:T(4,128)}, u32[]{:S(2)}) %copy-start.2) | copy-done | bytes 120
  3.0 0.0 copy-start.3
  3.0 0.7 %copy-done.3 = s32[4,2]{0,1:T(2,128)S(1)} copy-done((s32[4,2]{0,1:T(2,128)S(1)}, s32[4,2]{0,1:T(2,128)}, u32[]{:S(2)}) %copy-start.3) | copy-done | bytes 56
  3.7 0.0 copy-start.4
  3.7 0.7 %copy-done.4 = s32[8]{0:T(128)S(1)} copy-done((s32[8]{0:T(128)S(1)}, s32[8]{0:T(128)}, u32[]{:S(2)}) %copy-start.4) | copy-done | bytes 56
  4.4 27.3 %shard_map.55 = bf16[4,8,256,128]{3,2,1,0:T(8,128)(2,1)S(1)} custom-call(bf16[2,1536,128]{2,1,0:T(8,128)(2,1)S(1)} %bitcast.7, s32[3,8]{1,0:T(4,128)S(1)} %bitcast.8, s32[2,4]{1,0:T(2,128)S(1)} %bitcast.9, s32[8]{0:T(128)S(1)} %copy-done.4, bf16[4,64,2048]{2,1,0:T(8,128)(2,1)S(1)} %copy-done), custom_call_target="tpu_custom_call" | custom-call | tf_op jit(solution)/shard_map/pallas_call | solution.py:270
  31.7 1.3 %copy.7 = bf16[4,8,16,16,128]{4,3,2,1,0:T(8,128)(2,1)} copy(bf16[4,8,16,16,128]{4,3,2,1,0:T(8,128)(2,1)S(1)} %bitcast.6) | data formatting | bytes 4194304
Async XLA Ops:
  0.0 1.2 %copy-start = (bf16[4,64,2048]{2,1,0:T(8,128)(2,1)S(1)}, bf16[4,64,2048]{2,1,0:T(8,128)(2,1)}, u32[]{:S(2)}) copy-start(bf16[4,64,2048]{2,1,0:T(8,128)(2,1)} %tau.1) | copy-start | bytes 3145732
  1.2 1.1 %copy-start.1 = (bf16[2,512,3,128]{3,1,2,0:T(8,128)(2,1)S(1)}, bf16[2,512,3,128]{3,1,2,0:T(8,128)(2,1)}, u32[]{:S(2)}) copy-start(bf16[2,512,3,128]{3,1,2,0:T(8,128)(2,1)} %param.5) | copy-start | bytes 2359300
  2.4 0.7 %copy-start.2 = (s32[8,3]{0,1:T(4,128)S(1)}, s32[8,3]{0,1:T(4,128)}, u32[]{:S(2)}) copy-start(s32[8,3]{0,1:T(4,128)} %param.6) | copy-start | bytes 292
  3.0 0.7 %copy-start.3 = (s32[4,2]{0,1:T(2,128)S(1)}, s32[4,2]{0,1:T(2,128)}, u32[]{:S(2)}) copy-start(s32[4,2]{0,1:T(2,128)} %param.7) | copy-start | bytes 100
  3.7 0.7 %copy-start.4 = (s32[8]{0:T(128)S(1)}, s32[8]{0:T(128)}, u32[]{:S(2)}) copy-start(s32[8]{0:T(128)} %slots.1) | copy-start | bytes 100

commit v2 on v1

--- a/solution.py
+++ b/solution.py
@@ -42,18 +42,25 @@
 
 
 def kernel(
-    dims, eig, momenta, pairs, slots, tau, out,
-    cos_tab, sin_tab, turned, part, arrived, sinks, sources, right, half,
+    dims, eig_hbm, momenta_hbm, pairs_hbm, slots_hbm, sinks, sources,
+    eig, momenta, pairs, slots, in_sem,
+    cos_tab, sin_tab, turned, part, arrived,
     rs_send, rs_recv, z_send, z_recv, own_send, own_recv, core_send, core_recv, fwd_send, fwd_recv,
     *gathered,
 ):
     n_t, n_x, n_p, chunks, site_count, colours = dims
+    fetches = [
+        pltpu.make_async_copy(source, target, in_sem.at[index])
+        for index, (source, target) in enumerate((
+            (momenta_hbm, momenta), (eig_hbm, eig), (pairs_hbm, pairs), (slots_hbm, slots)))
+    ]
+    for fetch in fetches:
+        fetch.start()
     group = n_x * n_p
     slices = eig.shape[0]
     moms = momenta.shape[1]
-    pair_count, vectors = tau.shape[0], tau.shape[1]
-    width = 2 * vectors
-    spins = tau.shape[2] // width
+    pair_count, width = pairs.shape[1], eig.shape[2]
+    vectors = width // 2
     per = moms // chunks
     share = vectors // group
     rows = per * share
@@ -70,6 +77,7 @@
         other = lax.rem(pos + d, group)
         return other, {"space": lax.div(other, n_p), "spin": lax.rem(other, n_p)}
 
+    fetches[0].wait()
     cos_value, sin_value = phase_tables(momenta, pos * site_count, site_count, moms)
     cos_tab[...] = cos_value
     sin_tab[...] = sin_value
@@ -168,37 +176,41 @@
             sinks[ch, k] = gathered[ch][slots[pairs[0, k]]]
             sources[ch, pos, k] = gathered[ch][slots[pairs[1, k]]]
 
-    def prepare(k, carry):
-        right[k, :vectors, :] = tau[k]
-        for g in range(spins):
-            block = tau[k, :, g * width : (g + 1) * width].astype(F32)
-            right[k, vectors:, g * width : (g + 1) * width] = (swap(block) * minus_first).astype(BF16)
-        return carry
-
-    def contract(ch):
-        def pair(k, carry):
-            halfway = jnp.dot(sinks[ch, k], right[k], preferred_element_type=F32)
-            for g in range(spins):
-                half[pl.ds(g, rows, stride=spins), :] = halfway[:, g * width : (g + 1) * width]
-            for mi in range(per):
-                q = jnp.concatenate(
-                    [sources[ch, g, k, mi * share : (mi + 1) * share, :] for g in range(group)], axis=0)
-                swapped = (swap(q.astype(F32)) * minus_first).astype(BF16)
-                conjugate = jnp.concatenate([q, swapped], axis=0)
-                left = half[mi * share * spins : (mi + 1) * share * spins, :].astype(BF16)
-                loops = lax.dot_general(
-                    left, conjugate, (((1,), (1,)), ((), ())), preferred_element_type=F32)
-                out[k, ch * per + mi] = loops.astype(BF16)
-            return carry
-
-        lax.fori_loop(0, pair_count, pair, 0)
-
     rs, zs, owns, fwds = {}, {}, {}, {}
     barrier = pltpu.get_barrier_semaphore()
     for d in range(1, group):
         pl.semaphore_signal(barrier, inc=1, device_id=peer(d)[1], device_id_type=MESH)
     for d in range(1, n_t):
         pl.semaphore_signal(barrier, inc=1, device_id={"tm": lax.rem(t + d, n_t)}, device_id_type=MESH)
+    fetches[1].wait()
+
+    def reduced(ch):
+        for copy in rs[ch]:
+            copy.wait_recv()
+        reduce_share(ch)
+        zs[ch] = z_copies(ch)
+        for copy in zs[ch]:
+            copy.start()
+
+    def selected(ch):
+        if ch == 0:
+            for fetch in fetches[2:]:
+                fetch.wait()
+        for copy in zs[ch]:
+            copy.wait_recv()
+        select(ch)
+        owns[ch] = own_copies(ch)
+        for copy in owns[ch][0] + owns[ch][1]:
+            copy.start()
+
+    def forwarded(ch):
+        fwds[ch] = []
+        for d in range(1, n_x):
+            owns[ch][0][d - 1].wait_recv()
+            fwds[ch].append(forward_copies(ch, d))
+            for copy in fwds[ch][-1]:
+                copy.start()
+
     for ch in range(chunks):
         compute(ch)
         if ch == 0:
@@ -207,41 +219,21 @@
         for copy in rs[ch]:
             copy.start()
         if ch >= 1:
-            for copy in rs[ch - 1]:
-                copy.wait_recv()
-            reduce_share(ch - 1)
-            zs[ch - 1] = z_copies(ch - 1)
-            for copy in zs[ch - 1]:
-                copy.start()
-    lax.fori_loop(0, pair_count, prepare, 0)
-    last = chunks - 1
-    for copy in rs[last]:
-        copy.wait_recv()
-    reduce_share(last)
-    zs[last] = z_copies(last)
-    for copy in zs[last]:
-        copy.start()
-    for ch in range(chunks):
-        for copy in zs[ch]:
-            copy.wait_recv()
-        select(ch)
-        owns[ch] = own_copies(ch)
-        for copy in owns[ch][0] + owns[ch][1]:
-            copy.start()
-    for ch in range(chunks):
-        fwds[ch] = []
-        for d in range(1, n_x):
-            owns[ch][0][d - 1].wait_recv()
-            fwds[ch].append(forward_copies(ch, d))
-            for copy in fwds[ch][-1]:
-                copy.start()
+            reduced(ch - 1)
+        if ch >= 3:
+            selected(ch - 3)
+    reduced(chunks - 1)
+    for ch in range(max(chunks - 3, 0), chunks):
+        selected(ch)
+        if ch >= 1:
+            forwarded(ch - 1)
+    forwarded(chunks - 1)
     for ch in range(chunks):
         for copy in owns[ch][1]:
             copy.wait_recv()
         for group_copies in fwds[ch]:
             for copy in group_copies:
                 copy.wait_recv()
-        contract(ch)
     for ch in range(chunks):
         for copy in rs[ch] + zs[ch] + owns[ch][0] + owns[ch][1]:
             copy.wait_send()
@@ -250,7 +242,39 @@
                 copy.wait_send()
 
 
-CHUNKS = 2
+def contraction(sinks, sources, tau, out, right, half):
+    chunks, group, rows, width = sources.shape[0], sources.shape[1], sources.shape[3], sources.shape[4]
+    vectors = width // 2
+    spins = tau.shape[2] // width
+    share = vectors // group
+    per = rows // share
+    lane = lax.broadcasted_iota(jnp.int32, (1, width), 1)
+    minus_first = jnp.where(lane < vectors, -1.0, 1.0).astype(F32)
+
+    right[:vectors, :] = tau[0]
+    for g in range(spins):
+        block = tau[0, :, g * width : (g + 1) * width].astype(F32)
+        right[vectors:, g * width : (g + 1) * width] = (
+            pltpu.roll(block, vectors, 1) * minus_first).astype(BF16)
+    left = sinks[:, 0].reshape(chunks * rows, width)
+    for g in range(0, spins, 2):
+        halfway = jnp.dot(left, right[:, g * width : (g + 2) * width], preferred_element_type=F32)
+        for e in range(2):
+            half[pl.ds(g + e, chunks * rows, stride=spins), :] = halfway[:, e * width : (e + 1) * width]
+    block_rows = share * spins
+    for ch in range(chunks):
+        for mi in range(per):
+            m = ch * per + mi
+            q = jnp.concatenate(
+                [sources[ch, g, 0, mi * share : (mi + 1) * share, :] for g in range(group)], axis=0)
+            swapped = (pltpu.roll(q.astype(F32), vectors, 1) * minus_first).astype(BF16)
+            conjugate = jnp.concatenate([q, swapped], axis=0)
+            out[0, m] = lax.dot_general(
+                half[m * block_rows : (m + 1) * block_rows, :].astype(BF16), conjugate,
+                (((1,), (1,)), ((), ())), preferred_element_type=F32).astype(BF16)
+
+
+CHUNKS = 4
 
 
 def per_device(eigenvectors, momenta, time_pairs, slot_map, perambulators):
@@ -265,23 +289,27 @@
     rows = per * share
     eig = jnp.transpose(eigenvectors, (0, 2, 1, 3)).reshape(slices, colours * site_count, width)
     vmem = pl.BlockSpec(memory_space=pltpu.VMEM)
-    smem = pl.BlockSpec(memory_space=pltpu.SMEM)
+    hbm = pl.BlockSpec(memory_space=pltpu.HBM)
     dma = pltpu.SemaphoreType.DMA
-    out = pl.pallas_call(
+    sinks, sources = pl.pallas_call(
         functools.partial(kernel, (n_t, n_x, n_p, CHUNKS, site_count, colours)),
-        out_shape=jax.ShapeDtypeStruct((pair_count, moms, share * spins, width), BF16),
-        in_specs=[vmem, smem, smem, smem, vmem],
-        out_specs=vmem,
+        out_shape=[
+            jax.ShapeDtypeStruct((CHUNKS, pair_count, rows, width), BF16),
+            jax.ShapeDtypeStruct((CHUNKS, group, pair_count, rows, width), BF16),
+        ],
+        in_specs=[hbm] * 4,
+        out_specs=[vmem, vmem],
         scratch_shapes=[
+            pltpu.VMEM(eig.shape, BF16),
+            pltpu.SMEM((momenta.shape[1], moms), jnp.int32),
+            pltpu.SMEM((2, pair_count), jnp.int32),
+            pltpu.SMEM(slot_map.shape, jnp.int32),
+            dma((4,)),
             pltpu.VMEM((site_count, 128), F32),
             pltpu.VMEM((site_count, 128), F32),
             pltpu.VMEM((slices, colours * site_count, per * width), BF16),
             pltpu.VMEM((CHUNKS, group, slices * rows, width), BF16),
             pltpu.VMEM((CHUNKS, group - 1, slices * rows, width), BF16),
-            pltpu.VMEM((CHUNKS, pair_count, rows, width), BF16),
-            pltpu.VMEM((CHUNKS, group, pair_count, rows, width), BF16),
-            pltpu.VMEM((pair_count, width, columns), BF16),
-            pltpu.VMEM((rows * spins, width), F32),
             dma((CHUNKS, group - 1)), dma((CHUNKS, group - 1)),
             dma((CHUNKS, n_t - 1)), dma((CHUNKS, n_t - 1)),
             dma((CHUNKS, n_x - 1)), dma((CHUNKS, n_x - 1)),
@@ -289,9 +317,28 @@
             dma((CHUNKS, n_x - 1, n_p - 1)), dma((CHUNKS, n_x - 1, n_p - 1)),
         ] + [pltpu.VMEM((n_t * slices, rows, width), BF16)] * CHUNKS,
         compiler_params=pltpu.CompilerParams(
-            collective_id=0, has_side_effects=True, vmem_limit_bytes=40 * 1024 * 1024),
-    )(eig, momenta.T, time_pairs.T, slot_map, perambulators)
+            collective_id=0, has_side_effects=True, vmem_limit_bytes=VMEM_MIB * 1024 * 1024),
+    )(eig, momenta.T, time_pairs.T, slot_map)
+    out = pl.pallas_call(
+        contraction,
+        grid=(pair_count,),
+        out_shape=jax.ShapeDtypeStruct((pair_count, moms, share * spins, width), BF16),
+        in_specs=[
+            pl.BlockSpec((CHUNKS, 1, rows, width), lambda k: (0, k, 0, 0)),
+            pl.BlockSpec((CHUNKS, group, 1, rows, width), lambda k: (0, 0, k, 0, 0)),
+            pl.BlockSpec((1, vectors, columns), lambda k: (k, 0, 0)),
+        ],
+        out_specs=pl.BlockSpec((1, moms, share * spins, width), lambda k: (k, 0, 0, 0)),
+        scratch_shapes=[
+            pltpu.VMEM((width, columns), BF16),
+            pltpu.VMEM((moms * share * spins, width), F32),
+        ],
+        compiler_params=pltpu.CompilerParams(vmem_limit_bytes=VMEM_MIB * 1024 * 1024),
+    )(sinks, sources, perambulators)
     return out.reshape(pair_count, moms, share, spins, width)
+
+
+VMEM_MIB = 63
 
 
 def solution(mesh):

time: 33.3 us -> 36.2 us (1.087)
  Pallas kernels: 27.3 us -> 36 us
  local copies, waits for them, and re-layouts: 5.69 us -> 0 us
    unnamed x11 -> x0, local copies, waits for them, and re-layouts: 5.69 us -> none
    pallas_call x0 -> x1, Pallas kernels: none -> 5.52 us  [per_device(): pl.pallas_call(contraction, grid=(pair_count,), out_shape=jax.ShapeDtypeS...]
    pallas_call x1, Pallas kernels: 27.3 us -> 30.5 us  [per_device(): pl.pallas_call(functools.partial(kernel, (n_t, n_x, n_p, CHUNKS, site_cou...]
where the time goes in v2:
time: 36.2 us; the launch traced here: 36 us
  Pallas kernels  36 us (99%)
    pallas_call x1, Pallas kernels, per_device(): pl.pallas_call(functools.partial(kernel, (n_t, n_x, n_p, CHUNKS, site_cou...  30.5 us
    pallas_call x1, Pallas kernels, per_device(): pl.pallas_call(contraction, grid=(pair_count,), out_shape=jax.ShapeDtypeS...  5.52 us

profile of v2, /device:TPU:0, one launch (start us, length us, event | category | flops | bytes accessed | tf_op | source)
XLA Modules:
  0.0 36.0 jit_solution(10990068030398262531)
XLA Ops:
  0.0 30.5 %shard_map.55 = (bf16[4,4,32,128]{3,2,1,0:T(8,128)(2,1)}, bf16[4,4,4,32,128]{4,3,2,1,0:T(8,128)(2,1)}) custom-call(bf16[2,1536,128]{2,1,0:T(8,128)(2,1)} %bitcast.6, s32[3,8]{1,0:T(4,128)} %bitcast.7, s32[2,4]{1,0:T(2,128)} %bitcast.8, s32[8]{0:T(128)} %slots_hbm.1), custom_call_target="tpu_custom_call" | custom-call | tf_op jit(solution)/shard_map/pallas_call | solution.py:294
  30.5 5.5 %shard_map.56 = bf16[4,8,256,128]{3,2,1,0:T(8,128)(2,1)} custom-call(bf16[4,4,32,128]{3,2,1,0:T(8,128)(2,1)} %get-tuple-element.7.sinks, bf16[4,4,4,32,128]{4,3,2,1,0:T(8,128)(2,1)} %get-tuple-element.8.sources, bf16[4,64,2048]{2,1,0:T(8,128)(2,1)} %tau.1), custom_call_target="tpu_custom_call" | custom-call | tf_op jit(solution)/shard_map/pallas_call | solution.py:322

commit v3 on v2

--- a/solution.py
+++ b/solution.py
@@ -82,7 +82,7 @@
     cos_tab[...] = cos_value
     sin_tab[...] = sin_value
 
-    step = 16
+    step = STEP
 
     def compute(ch):
         def block(i, carry):
@@ -104,7 +104,7 @@
                     ).astype(BF16)
             return carry
 
-        lax.fori_loop(0, site_count // step, block, 0)
+        lax.fori_loop(0, site_count // step, block, 0, unroll=UNROLL)
         for r in range(slices):
             product = lax.dot_general(
                 eig[r], turned[r], (((0,), (0,)), ((), ())), preferred_element_type=F32
@@ -274,7 +274,9 @@
                 (((1,), (1,)), ((), ())), preferred_element_type=F32).astype(BF16)
 
 
-CHUNKS = 4
+CHUNKS = 2
+STEP = 16
+UNROLL = 8
 
 
 def per_device(eigenvectors, momenta, time_pairs, slot_map, perambulators):

time: 36.2 us -> 27.1 us (0.75)
  Pallas kernels: 36 us -> 26.9 us
    pallas_call x1, Pallas kernels: 30.5 us -> 21.3 us  [per_device(): pl.pallas_call(functools.partial(kernel, (n_t, n_x, n_p, CHUNKS, site_cou...]
where the time goes in v3:
time: 27.1 us; the launch traced here: 26.9 us
  Pallas kernels  26.9 us (99%)
    pallas_call x1, Pallas kernels, per_device(): pl.pallas_call(functools.partial(kernel, (n_t, n_x, n_p, CHUNKS, site_cou...  21.3 us
    pallas_call x1, Pallas kernels, per_device(): pl.pallas_call(contraction, grid=(pair_count,), out_shape=jax.ShapeDtypeS...  5.52 us

profile of v3, /device:TPU:0, one launch (start us, length us, event | category | flops | bytes accessed | tf_op | source)
XLA Modules:
  0.0 26.9 jit_solution(12399500191034421756)
XLA Ops:
  0.0 21.3 %shard_map.55 = (bf16[2,4,64,128]{3,2,1,0:T(8,128)(2,1)}, bf16[2,4,4,64,128]{4,3,2,1,0:T(8,128)(2,1)}) custom-call(bf16[2,1536,128]{2,1,0:T(8,128)(2,1)} %bitcast.6, s32[3,8]{1,0:T(4,128)} %bitcast.7, s32[2,4]{1,0:T(2,128)} %bitcast.8, s32[8]{0:T(128)} %slots_hbm.1), custom_call_target="tpu_custom_call" | custom-call | tf_op jit(solution)/shard_map/pallas_call | solution.py:296
  21.4 5.5 %shard_map.56 = bf16[4,8,256,128]{3,2,1,0:T(8,128)(2,1)} custom-call(bf16[2,4,64,128]{3,2,1,0:T(8,128)(2,1)} %get-tuple-element.7.sinks, bf16[2,4,4,64,128]{4,3,2,1,0:T(8,128)(2,1)} %get-tuple-element.8.sources, bf16[4,64,2048]{2,1,0:T(8,128)(2,1)} %tau.1), custom_call_target="tpu_custom_call" | custom-call | tf_op jit(solution)/shard_map/pallas_call | solution.py:324
